TPU v7x, 32 devices: a whole 2x2x4 slice. The times are simulated.
32 devices in a mesh: parts: 2 (over x), gx: 8 (over z, y), gy: 2 (over core).
Axes of the slice: x: 2, y: 2, z: 4, core: 2. Of those that a mesh axis runs over, the one named last changes fastest.
Arguments:
- features: bfloat16 [128, 512, 128], P(('parts', 'gx', 'gy')), parts along dimension 0, may hold values from -6 to 6
- cotangent: bfloat16 [128, 512, 128], P(('parts', 'gx', 'gy')), parts along dimension 0, may hold values from -6 to 6
- weights: bfloat16 [27, 128, 128], replicated, may hold values from -0.109375 to 0.109375
- neighbours: int32 [128, 27], P(('parts', 'gx', 'gy')), parts along dimension 0, may hold values from -1 to 63, as said below
- counts: int32 [32], P(('parts', 'gx', 'gy')), parts along dimension 0, may hold values from 2 to 4, as said below
Outputs:
- outputs: bfloat16 [128, 512, 128], P(('parts', 'gx', 'gy')), parts along dimension 0
- feature_grad: bfloat16 [128, 512, 128], P(('parts', 'gx', 'gy')), parts along dimension 0
- weight_grad: float32 [6912, 128], P('parts'), parts along dimension 0
There are 2 independent parts, one for each index of `parts`. A program takes and returns all parts, laid end to end along the dimension named above; an argument that names none is the same for every part. Nothing has to cross between parts.
Inputs may be any that keep to these rules, and one draw needn't show every extreme that they name: `neighbours`: entries are -1 or the slot id of a live brick; the brick's device is at most one step away along gx and at most one along gy. The relation is symmetric, entry 13 of a live slot is the slot itself, and every row of a slot that is not live is all -1. `counts`: A device's live bricks are its first slots; some devices hold 4.
All inputs are finite; a program needn't handle non-finite values.
Results may differ from a plain program's by a relative error of at most 0.001.
Values may be sent and summed in bfloat16 or wider, within the bound.
A program may use at most 128 MiB of HBM per device.

v0:
```python
import functools

import jax
import jax.numpy as jnp
from jax import lax
from jax.experimental import pallas as pl
from jax.experimental.pallas import tpu as pltpu
from jax.sharding import PartitionSpec as P

MESH = pl.DeviceIdType.MESH
F32 = jnp.float32
BF16 = jnp.bfloat16


def kernel(
    n_gx,
    reduce_here,
    nb_ref,
    counts_ref,
    f_ref,
    g_ref,
    w_ref,
    out_ref,
    grad_ref,
    dw_ref,
    table_f,
    table_g,
    x_f,
    x_g,
    m_cat,
    w_back,
    acc,
    idx,
    part,
    got_core,
    got_y,
    got_z,
    own_sem,
    halo_send,
    halo_recv,
    red_send,
    red_recv,
):
    slots = f_ref.shape[0]
    tables = (table_f, table_g)
    nothing = 9 * slots
    rank = lax.axis_index("parts")
    gx = lax.axis_index("gx")
    gy = lax.axis_index("gy")
    other = 1 - gy
    up, down = lax.rem(gx + 1, n_gx), lax.rem(gx + n_gx - 1, n_gx)

    partners = [(up, gy), (down, gy), (gx, other), (up, other), (down, other)]
    if reduce_here:
        partners += [(lax.rem(gx + 2 * d, n_gx), gy) for d in (1, 2, 3)]
    barrier = pltpu.get_barrier_semaphore()
    for x, y in partners:
        pl.semaphore_signal(barrier, inc=1, device_id=(rank, x, y), device_id_type=MESH)

    own = [
        pltpu.make_async_copy(
            ref, tables[field].at[pl.ds(4 * slots, slots)], own_sem.at[field]
        )
        for field, ref in enumerate((f_ref, g_ref))
    ]
    for copy in own:
        copy.start()
    pl.semaphore_wait(barrier, len(partners))

    line = pl.ds(pl.multiple_of(48 * other, 16), 16)
    has_up, has_down = gx < n_gx - 1, gx > 0

    def halo(field, ref, kind):
        table = tables[field]
        if kind == 0:
            source = ref.at[:, 7]
            target = table.at[pl.ds(1 * slots, slots), 7]
            device = (rank, up, gy)
        elif kind == 1:
            source = ref.at[:, 0]
            target = table.at[pl.ds(7 * slots, slots), 0]
            device = (rank, down, gy)
        elif kind == 2:
            source = ref.at[:, :, line]
            target = table.at[pl.ds((3 + 2 * gy) * slots, slots), :, line]
            device = (rank, gx, other)
        elif kind == 3:
            source = ref.at[:, 7, line]
            target = table.at[pl.ds(2 * gy * slots, slots), 7, line]
            device = (rank, up, other)
        else:
            source = ref.at[:, 0, line]
            target = table.at[pl.ds((6 + 2 * gy) * slots, slots), 0, line]
            device = (rank, down, other)
        return pltpu.make_async_remote_copy(
            src_ref=source,
            dst_ref=target,
            send_sem=halo_send.at[field, kind],
            recv_sem=halo_recv.at[field, kind],
            device_id=device,
            device_id_type=MESH,
        )

    copies = [[halo(field, ref, kind) for kind in range(5)] for field, ref in enumerate((f_ref, g_ref))]

    def start(field):
        @pl.when(has_up)
        def _():
            copies[field][0].start()
            copies[field][3].start()

        @pl.when(has_down)
        def _():
            copies[field][1].start()
            copies[field][4].start()

        copies[field][2].start()

    def arrived(field):
        @pl.when(has_down)
        def _():
            copies[field][0].wait_recv()
            copies[field][3].wait_recv()

        @pl.when(has_up)
        def _():
            copies[field][1].wait_recv()
            copies[field][4].wait_recv()

        copies[field][2].wait_recv()

    def sent(field):
        @pl.when(has_up)
        def _():
            copies[field][0].wait_send()
            copies[field][3].wait_send()

        @pl.when(has_down)
        def _():
            copies[field][1].wait_send()
            copies[field][4].wait_send()

        copies[field][2].wait_send()

    start(0)
    start(1)

    def fill(n, carry):
        s, o = n // 27, n % 27
        entry = nb_ref[s, o]
        safe = jnp.maximum(entry, 0)
        owner = safe // slots
        relative = (owner // 2 - gx + 1) * 3 + (owner % 2 - gy + 1)
        place = jnp.where(entry < 0, nothing, relative * slots + safe % slots)
        idx[s, o] = jnp.minimum(jnp.maximum(place, 0), nothing)
        return carry

    lax.fori_loop(0, 27 * slots, fill, 0)

    for field in range(2):
        tables[field][nothing] = jnp.zeros(table_f.shape[1:], BF16)

    def turn(o, carry):
        rows = pl.ds(pl.multiple_of(o * 128, 128), 128)
        w_back[rows, :] = w_ref[26 - o].astype(F32).T.astype(BF16)
        return carry

    lax.fori_loop(0, 27, turn, 0)

    for copy in own:
        copy.wait()

    def spread(s, carry):
        base = pl.multiple_of(s * 640, 128)
        value = table_g[4 * slots + s].reshape(512, 128)
        value = jnp.where(s < counts_ref[0], value.astype(F32), 0.0).astype(BF16)
        for a in range(3):
            columns = slice(a * 128, a * 128 + 128)
            if a > 0:
                m_cat[pl.ds(base, a * 64), columns] = jnp.zeros((a * 64, 128), BF16)
            if a < 2:
                m_cat[pl.ds(base + a * 64 + 512, 128 - a * 64), columns] = jnp.zeros(
                    (128 - a * 64, 128), BF16
                )
            m_cat[pl.ds(base + a * 64, 512), columns] = value
        return carry

    lax.fori_loop(0, slots, spread, 0)

    sub = lax.broadcasted_iota(jnp.int32, (10, 8, 128), 1)

    def build(table, x_ref):
        def plane(n, carry):
            s, p = n // 10, n % 10
            first = jnp.where(p == 0, 0, jnp.where(p == 9, 18, 9))
            i = (p + 7) % 8

            def gathered(z):
                low = table[idx[s, first + z], i, 48:64].astype(F32)[8:]
                mid = table[idx[s, first + 3 + z], i].astype(F32)
                high = table[idx[s, first + 6 + z], i, 0:16].astype(F32)[:8]
                return jnp.concatenate([low, mid, high], axis=0).reshape(10, 8, 128)

            below, here, above = gathered(0), gathered(1), gathered(2)
            lower = pltpu.roll(jnp.where(sub == 7, below, here), 1, 1)
            upper = pltpu.roll(jnp.where(sub == 0, above, here), 7, 1)
            rows = pl.ds(pl.multiple_of(n * 64, 64), 64)
            for c, value in enumerate((lower, here, upper)):
                for b in range(3):
                    o = b * 3 + c
                    x_ref[rows, o * 128 : o * 128 + 128] = (
                        value[b : b + 8].reshape(64, 128).astype(BF16)
                    )
            return carry

        lax.fori_loop(0, 10 * slots, plane, 0)

    def product(x_ref, weight, result):
        def brick(s, carry):
            total = jnp.zeros((512, 128), F32)
            for a in range(3):
                rows = pl.ds(pl.multiple_of(s * 640 + a * 64, 64), 512)
                total += jnp.dot(
                    x_ref[rows, :],
                    weight[a * 1152 : a * 1152 + 1152, :],
                    preferred_element_type=F32,
                )
            result[s] = jnp.where(s < counts_ref[0], total, 0.0).astype(BF16)
            return carry

        lax.fori_loop(0, slots, brick, 0)

    def outer(t):
        acc[...] = jnp.zeros_like(acc)

        def brick(s, carry):
            rows = pl.ds(pl.multiple_of(s * 640, 128), 640)
            acc[...] += lax.dot_general(
                x_f[rows, t * 384 : t * 384 + 384],
                m_cat[rows, :],
                (((0,), (0,)), ((), ())),
                preferred_element_type=F32,
            )
            return carry

        lax.fori_loop(0, slots, brick, 0)
        target = part if reduce_here else dw_ref
        for a in range(3):
            for c in range(3):
                block = acc[c * 128 : c * 128 + 128, a * 128 : a * 128 + 128]
                target[a, t, c] = block.reshape(16, 8, 128)

    w_flat = w_ref.reshape(27 * 128, 128)

    arrived(0)
    build(table_f, x_f)
    if not reduce_here:
        for t in range(3):
            outer(t)
        arrived(1)
        build(table_g, x_g)
        product(x_f, w_flat, out_ref)
        product(x_g, w_back, grad_ref)
        sent(0)
        sent(1)
        return

    z, y = gx // 2, gx % 2
    half = 8 * gy
    quarter = half + 4 * y
    share = quarter + z
    side = (rank, z * 2 + 1 - y, gy)
    depth = [lax.rem(z + d, 4) for d in (1, 2, 3)]

    def send(t, k, source, target, device):
        return pltpu.make_async_remote_copy(
            src_ref=source,
            dst_ref=target,
            send_sem=red_send.at[t, k],
            recv_sem=red_recv.at[t, k],
            device_id=device,
            device_id_type=MESH,
        )

    core_step, y_step, z_step, z_back, y_back, core_back = [], [], [], [], [], []
    for t in range(3):
        core_step.append(
            send(t, 0, part.at[:, t, :, pl.ds(8 * other, 8)], got_core.at[t], (rank, gx, other))
        )
        y_step.append(
            send(t, 1, part.at[:, t, :, pl.ds(half + 4 * (1 - y), 4)], got_y.at[t], side)
        )
        z_step.append(
            [
                send(
                    t,
                    2 + d,
                    part.at[:, t, :, quarter + depth[d]],
                    got_z.at[t, d],
                    (rank, depth[d] * 2 + y, gy),
                )
                for d in range(3)
            ]
        )
        mine = dw_ref.at[:, t, :, share]
        z_back.append(
            [send(t, 5 + d, mine, mine, (rank, depth[d] * 2 + y, gy)) for d in range(3)]
        )
        mine = dw_ref.at[:, t, :, pl.ds(quarter, 4)]
        y_back.append(send(t, 8, mine, mine, side))
        mine = dw_ref.at[:, t, :, pl.ds(half, 8)]
        core_back.append(send(t, 9, mine, mine, (rank, gx, other)))

    def after_core(t):
        core_step[t].wait_recv()
        for a in range(3):
            for c in range(3):
                part[a, t, c, pl.ds(half, 8)] += got_core[t, a, c]
        y_step[t].start()

    def after_y(t):
        y_step[t].wait_recv()
        for a in range(3):
            for c in range(3):
                part[a, t, c, pl.ds(quarter, 4)] += got_y[t, a, c]
        for copy in z_step[t]:
            copy.start()

    def after_z(t):
        for copy in z_step[t]:
            copy.wait_recv()
        for a in range(3):
            for c in range(3):
                dw_ref[a, t, c, share] = (part[a, t, c, share] + got_z[t, 0, a, c]) + (
                    got_z[t, 1, a, c] + got_z[t, 2, a, c]
                )
        for copy in z_back[t]:
            copy.start()

    def after_z_back(t):
        for copy in z_back[t]:
            copy.wait_recv()
        y_back[t].start()

    def after_y_back(t):
        y_back[t].wait_recv()
        core_back[t].start()

    outer(0)
    core_step[0].start()
    outer(1)
    core_step[1].start()
    after_core(0)
    outer(2)
    core_step[2].start()
    after_core(1)
    arrived(1)
    build(table_g, x_g)
    after_core(2)
    after_y(0)
    product(x_f, w_flat, out_ref)
    after_y(1)
    after_z(0)
    after_y(2)
    product(x_g, w_back, grad_ref)
    after_z(1)
    after_z_back(0)
    after_z(2)
    after_z_back(1)
    after_y_back(0)
    after_z_back(2)
    after_y_back(1)
    after_y_back(2)
    for t in range(3):
        core_back[t].wait_recv()
    sent(0)
    sent(1)
    for t in range(3):
        for copy in [core_step[t], y_step[t], *z_step[t], *z_back[t], y_back[t], core_back[t]]:
            copy.wait_send()


def body(n_gx, features, cotangent, weights, neighbours, counts):
    slots, voxels, channels = features.shape
    reduce_here = n_gx == 8
    any_space = pl.BlockSpec(memory_space=pl.ANY)
    vmem = pl.BlockSpec(memory_space=pltpu.VMEM)
    smem = pl.BlockSpec(memory_space=pltpu.SMEM)
    rows = slots * 640
    outputs, grad, weight_grad = pl.pallas_call(
        functools.partial(kernel, n_gx, reduce_here),
        out_shape=(
            jax.ShapeDtypeStruct((slots, voxels, channels), BF16),
            jax.ShapeDtypeStruct((slots, voxels, channels), BF16),
            jax.ShapeDtypeStruct((3, 3, 3, 16, 8, channels), F32),
        ),
        in_specs=[smem, smem, any_space, any_space, vmem],
        out_specs=(vmem, vmem, vmem),
        scratch_shapes=[
            pltpu.VMEM((9 * slots + 1, 8, 64, channels), BF16),
            pltpu.VMEM((9 * slots + 1, 8, 64, channels), BF16),
            pltpu.VMEM((rows, 9 * channels), BF16),
            pltpu.VMEM((rows, 9 * channels), BF16),
            pltpu.VMEM((rows, 3 * channels), BF16),
            pltpu.VMEM((27 * channels, channels), BF16),
            pltpu.VMEM((3 * channels, 3 * channels), F32),
            pltpu.SMEM((slots, 27), jnp.int32),
            pltpu.VMEM((3, 3, 3, 16, 8, channels), F32),
            pltpu.VMEM((3, 3, 3, 8, 8, channels), F32),
            pltpu.VMEM((3, 3, 3, 4, 8, channels), F32),
            pltpu.VMEM((3, 3, 3, 3, 8, channels), F32),
            pltpu.SemaphoreType.DMA((2,)),
            pltpu.SemaphoreType.DMA((2, 5)),
            pltpu.SemaphoreType.DMA((2, 5)),
            pltpu.SemaphoreType.DMA((3, 10)),
            pltpu.SemaphoreType.DMA((3, 10)),
        ],
        compiler_params=pltpu.CompilerParams(
            collective_id=0, has_side_effects=True, vmem_limit_bytes=56 * 2**20
        ),
        cost_estimate=pl.CostEstimate(
            flops=6 * 27 * slots * voxels * channels * channels,
            bytes_accessed=8 * slots * voxels * channels,
            transcendentals=0,
        ),
    )(
        neighbours,
        counts,
        features.reshape(slots, 8, 64, channels),
        cotangent.reshape(slots, 8, 64, channels),
        weights,
    )
    weight_grad = weight_grad.reshape(27 * channels, channels)
    if not reduce_here:
        weight_grad = lax.psum(weight_grad, ("gx", "gy"))
    return outputs, grad, weight_grad


def solution(mesh):
    return jax.shard_map(
        functools.partial(body, mesh.shape["gx"]),
        mesh=mesh,
        in_specs=(
            P(("parts", "gx", "gy"), None, None),
            P(("parts", "gx", "gy"), None, None),
            P(),
            P(("parts", "gx", "gy"), None),
            P(("parts", "gx", "gy")),
        ),
        out_specs=(
            P(("parts", "gx", "gy"), None, None),
            P(("parts", "gx", "gy"), None, None),
            P("parts", None),
        ),
        check_vma=False,
    )
```

profile of v0, /device:TPU:0, one launch (start us, length us, event | category | flops | bytes accessed | tf_op | source)
XLA Modules:
  0.0 60.9 jit_solution(13685197108235804595)
XLA Ops:
  1.3 54.5 %shard_map.76 = (bf16[4,512,128]{2,1,0:T(8,128)(2,1)}, bf16[4,512,128]{2,1,0:T(8,128)(2,1)}, f32[3,3,3,16,8,128]{5,4,3,2,1,0:T(8,128)}) custom-call(s32[4,27]{1,0:T(4,128)} %nb_ref.1, s32[1]{0:T(128)S(6)} %copy.11.counts_ref, bf16[4,8,64,128]{3,2,1,0:T(8,128)(2,1)} %bitcast.4, bf16[4,8,64,128]{3,2,1,0:T(8,128)(2,1)} %bitcast.5, bf16[27,128,128]{2,1,0:T(8,128)(2,1)} %w_ref.1), custom_call_target="tpu_custom_call" | custom-call | flops 5435817984 | bytes 2097152 | tf_op jit(solution)/shard_map/pallas_call | solution.py:390
  55.8 0.0 copy-start
  55.8 2.0 %copy.12 = bf16[4,512,128]{2,1,0:T(8,128)(2,1)} copy(bf16[4,512,128]{2,1,0:T(8,128)(2,1)} %get-tuple-element.12) | data formatting | bytes 1048576
  57.8 1.9 %copy.13 = bf16[4,512,128]{2,1,0:T(8,128)(2,1)} copy(bf16[4,512,128]{2,1,0:T(8,128)(2,1)} %get-tuple-element.13) | data formatting | bytes 1048576
  59.7 0.0 copy-done
  59.7 1.2 %copy.14 = f32[3456,128]{1,0:T(8,128)} copy(f32[3456,128]{1,0:T(8,128)S(1)} %bitcast.3) | data formatting | bytes 3538944
Async XLA Ops:
  55.8 3.9 %copy-start = (f32[3,3,3,16,8,128]{5,4,3,2,1,0:T(8,128)S(1)}, f32[3,3,3,16,8,128]{5,4,3,2,1,0:T(8,128)}, u32[]{:S(2)}) copy-start(f32[3,3,3,16,8,128]{5,4,3,2,1,0:T(8,128)} %get-tuple-element.8) | copy-start | bytes 5308420
where the time goes:
time: 61.1 us; the launch traced here: 60.9 us
  Pallas kernels  54.5 us (89%)
  local copies, waits for them, and re-layouts  5.08 us (8%)
  between operations  1.3 us (2%)
    pallas_call x1, Pallas kernels, body(): pl.pallas_call(functools.partial(kernel, n_gx, reduce_here), out_shape=(j...  54.5 us
    unnamed x5, local copies, waits for them, and re-layouts  5.08 us

commit v1 on v0

--- a/solution.py
+++ b/solution.py
@@ -10,6 +10,40 @@
 MESH = pl.DeviceIdType.MESH
 F32 = jnp.float32
 BF16 = jnp.bfloat16
+
+
+def encode(values):
+    largest = jnp.max(jnp.abs(values), axis=0, keepdims=True)
+    exponent = jnp.floor(jnp.log2(jnp.maximum(largest, 1e-30)) + 0.01) - 14.0
+    scaled = jnp.floor(values * jnp.exp2(-exponent) + 0.5)
+    both = jnp.concatenate([scaled, exponent], axis=0)
+    return both.astype(jnp.int32).reshape(80, 128).astype(jnp.int16)
+
+
+def decode(coded):
+    both = coded.astype(jnp.int32).astype(F32).reshape(10, 8, 128)
+    return both[:9] * jnp.exp2(both[9:])
+
+
+def finish(coded, q_ref, out_in, grad_in, out_ref, grad_ref, dw_ref, sem):
+    copies = []
+    for n in range(out_in.shape[0]):
+        for k, (source, target) in enumerate(((out_in, out_ref), (grad_in, grad_ref))):
+            copies.append(pltpu.make_async_copy(source.at[n], target.at[n], sem.at[k, n]))
+    for copy in copies:
+        copy.start()
+
+    def piece(share, carry):
+        for t in range(3):
+            values = decode(q_ref[t, share]) if coded else q_ref[t, share]
+            for a in range(3):
+                for c in range(3):
+                    dw_ref[a, t, c, share] = values[a * 3 + c]
+        return carry
+
+    lax.fori_loop(0, 16, piece, 0)
+    for copy in copies:
+        copy.wait()
 
 
 def kernel(
@@ -19,10 +53,13 @@
     counts_ref,
     f_ref,
     g_ref,
+    w_hbm,
+    out_hbm,
+    grad_hbm,
+    dw_ref,
     w_ref,
     out_ref,
     grad_ref,
-    dw_ref,
     table_f,
     table_g,
     x_f,
@@ -33,7 +70,9 @@
     idx,
     part,
     got_core,
+    y_out,
     got_y,
+    z_out,
     got_z,
     own_sem,
     halo_send,
@@ -44,6 +83,8 @@
     slots = f_ref.shape[0]
     tables = (table_f, table_g)
     nothing = 9 * slots
+    bits = slots.bit_length() - 1
+    assert slots == 1 << bits
     rank = lax.axis_index("parts")
     gx = lax.axis_index("gx")
     gy = lax.axis_index("gy")
@@ -65,6 +106,10 @@
     ]
     for copy in own:
         copy.start()
+    weights_in = pltpu.make_async_copy(w_hbm, w_ref, own_sem.at[2])
+    weights_in.start()
+    out_copy = pltpu.make_async_copy(out_ref, out_hbm, own_sem.at[3])
+    grad_copy = pltpu.make_async_copy(grad_ref, grad_hbm, own_sem.at[4])
     pl.semaphore_wait(barrier, len(partners))
 
     line = pl.ds(pl.multiple_of(48 * other, 16), 16)
@@ -143,29 +188,21 @@
         copies[field][2].wait_send()
 
     start(0)
-    start(1)
-
-    def fill(n, carry):
-        s, o = n // 27, n % 27
-        entry = nb_ref[s, o]
-        safe = jnp.maximum(entry, 0)
-        owner = safe // slots
-        relative = (owner // 2 - gx + 1) * 3 + (owner % 2 - gy + 1)
-        place = jnp.where(entry < 0, nothing, relative * slots + safe % slots)
-        idx[s, o] = jnp.minimum(jnp.maximum(place, 0), nothing)
+
+    def fill(s, carry):
+        for o in range(27):
+            entry = nb_ref[s, o]
+            safe = jnp.maximum(entry, 0)
+            owner = safe >> bits
+            relative = ((owner >> 1) - gx + 1) * 3 + ((owner & 1) - gy + 1)
+            place = jnp.where(entry < 0, nothing, relative * slots + (safe & (slots - 1)))
+            idx[s, o] = jnp.minimum(jnp.maximum(place, 0), nothing)
         return carry
 
-    lax.fori_loop(0, 27 * slots, fill, 0)
+    lax.fori_loop(0, slots, fill, 0)
 
     for field in range(2):
         tables[field][nothing] = jnp.zeros(table_f.shape[1:], BF16)
-
-    def turn(o, carry):
-        rows = pl.ds(pl.multiple_of(o * 128, 128), 128)
-        w_back[rows, :] = w_ref[26 - o].astype(F32).T.astype(BF16)
-        return carry
-
-    lax.fori_loop(0, 27, turn, 0)
 
     for copy in own:
         copy.wait()
@@ -187,14 +224,15 @@
 
     lax.fori_loop(0, slots, spread, 0)
 
+    def turn(o, carry):
+        rows = pl.ds(pl.multiple_of(o * 128, 128), 128)
+        w_back[rows, :] = w_ref[26 - o].astype(F32).T.astype(BF16)
+        return carry
+
     sub = lax.broadcasted_iota(jnp.int32, (10, 8, 128), 1)
 
     def build(table, x_ref):
-        def plane(n, carry):
-            s, p = n // 10, n % 10
-            first = jnp.where(p == 0, 0, jnp.where(p == 9, 18, 9))
-            i = (p + 7) % 8
-
+        def plane(s, p, first, i):
             def gathered(z):
                 low = table[idx[s, first + z], i, 48:64].astype(F32)[8:]
                 mid = table[idx[s, first + 3 + z], i].astype(F32)
@@ -204,16 +242,25 @@
             below, here, above = gathered(0), gathered(1), gathered(2)
             lower = pltpu.roll(jnp.where(sub == 7, below, here), 1, 1)
             upper = pltpu.roll(jnp.where(sub == 0, above, here), 7, 1)
-            rows = pl.ds(pl.multiple_of(n * 64, 64), 64)
+            rows = pl.ds(pl.multiple_of(s * 640 + p * 64, 64), 64)
             for c, value in enumerate((lower, here, upper)):
                 for b in range(3):
                     o = b * 3 + c
                     x_ref[rows, o * 128 : o * 128 + 128] = (
                         value[b : b + 8].reshape(64, 128).astype(BF16)
                     )
-            return carry
-
-        lax.fori_loop(0, 10 * slots, plane, 0)
+
+        def brick(s, carry):
+            plane(s, 0, 0, 7)
+            plane(s, 9, 18, 0)
+
+            def inner(i, carry):
+                plane(s, i + 1, 9, i)
+                return carry
+
+            return lax.fori_loop(0, 8, inner, carry)
+
+        lax.fori_loop(0, slots, brick, 0)
 
     def product(x_ref, weight, result):
         def brick(s, carry):
@@ -248,19 +295,26 @@
         for a in range(3):
             for c in range(3):
                 block = acc[c * 128 : c * 128 + 128, a * 128 : a * 128 + 128]
-                target[a, t, c] = block.reshape(16, 8, 128)
+                target[t, :, a * 3 + c] = block.reshape(16, 8, 128)
 
     w_flat = w_ref.reshape(27 * 128, 128)
 
     arrived(0)
+    start(1)
     build(table_f, x_f)
     if not reduce_here:
         for t in range(3):
             outer(t)
         arrived(1)
         build(table_g, x_g)
+        weights_in.wait()
         product(x_f, w_flat, out_ref)
+        out_copy.start()
+        lax.fori_loop(0, 27, turn, 0)
         product(x_g, w_back, grad_ref)
+        grad_copy.start()
+        out_copy.wait()
+        grad_copy.wait()
         sent(0)
         sent(1)
         return
@@ -285,55 +339,49 @@
     core_step, y_step, z_step, z_back, y_back, core_back = [], [], [], [], [], []
     for t in range(3):
         core_step.append(
-            send(t, 0, part.at[:, t, :, pl.ds(8 * other, 8)], got_core.at[t], (rank, gx, other))
-        )
-        y_step.append(
-            send(t, 1, part.at[:, t, :, pl.ds(half + 4 * (1 - y), 4)], got_y.at[t], side)
-        )
+            send(t, 0, part.at[t, pl.ds(8 * other, 8)], got_core.at[t], (rank, gx, other))
+        )
+        y_step.append(send(t, 1, y_out.at[t], got_y.at[t], side))
         z_step.append(
             [
-                send(
-                    t,
-                    2 + d,
-                    part.at[:, t, :, quarter + depth[d]],
-                    got_z.at[t, d],
-                    (rank, depth[d] * 2 + y, gy),
-                )
+                send(t, 2 + d, z_out.at[t, d], got_z.at[t, d], (rank, depth[d] * 2 + y, gy))
                 for d in range(3)
             ]
         )
-        mine = dw_ref.at[:, t, :, share]
+        mine = dw_ref.at[t, share]
         z_back.append(
             [send(t, 5 + d, mine, mine, (rank, depth[d] * 2 + y, gy)) for d in range(3)]
         )
-        mine = dw_ref.at[:, t, :, pl.ds(quarter, 4)]
+        mine = dw_ref.at[t, pl.ds(quarter, 4)]
         y_back.append(send(t, 8, mine, mine, side))
-        mine = dw_ref.at[:, t, :, pl.ds(half, 8)]
+        mine = dw_ref.at[t, pl.ds(half, 8)]
         core_back.append(send(t, 9, mine, mine, (rank, gx, other)))
 
     def after_core(t):
         core_step[t].wait_recv()
-        for a in range(3):
-            for c in range(3):
-                part[a, t, c, pl.ds(half, 8)] += got_core[t, a, c]
+        for j in range(4):
+            place = 4 * (1 - y) + j
+            y_out[t, j] = encode(part[t, half + place] + got_core[t, place])
         y_step[t].start()
+        for j in range(4):
+            place = 4 * y + j
+            part[t, half + place] += got_core[t, place]
 
     def after_y(t):
         y_step[t].wait_recv()
-        for a in range(3):
-            for c in range(3):
-                part[a, t, c, pl.ds(quarter, 4)] += got_y[t, a, c]
+        for d in range(3):
+            z_out[t, d] = encode(part[t, quarter + depth[d]] + decode(got_y[t, depth[d]]))
         for copy in z_step[t]:
             copy.start()
+        part[t, share] += decode(got_y[t, z])
 
     def after_z(t):
         for copy in z_step[t]:
             copy.wait_recv()
-        for a in range(3):
-            for c in range(3):
-                dw_ref[a, t, c, share] = (part[a, t, c, share] + got_z[t, 0, a, c]) + (
-                    got_z[t, 1, a, c] + got_z[t, 2, a, c]
-                )
+        dw_ref[t, share] = encode(
+            (part[t, share] + decode(got_z[t, 0]))
+            + (decode(got_z[t, 1]) + decode(got_z[t, 2]))
+        )
         for copy in z_back[t]:
             copy.start()
 
@@ -355,14 +403,18 @@
     core_step[2].start()
     after_core(1)
     arrived(1)
+    after_core(2)
     build(table_g, x_g)
-    after_core(2)
     after_y(0)
+    weights_in.wait()
     product(x_f, w_flat, out_ref)
+    out_copy.start()
     after_y(1)
     after_z(0)
     after_y(2)
+    lax.fori_loop(0, 27, turn, 0)
     product(x_g, w_back, grad_ref)
+    grad_copy.start()
     after_z(1)
     after_z_back(0)
     after_z(2)
@@ -373,6 +425,8 @@
     after_y_back(2)
     for t in range(3):
         core_back[t].wait_recv()
+    out_copy.wait()
+    grad_copy.wait()
     sent(0)
     sent(1)
     for t in range(3):
@@ -387,16 +441,21 @@
     vmem = pl.BlockSpec(memory_space=pltpu.VMEM)
     smem = pl.BlockSpec(memory_space=pltpu.SMEM)
     rows = slots * 640
-    outputs, grad, weight_grad = pl.pallas_call(
+    results = jax.ShapeDtypeStruct((slots, voxels, channels), BF16)
+    sums = (3, 16, 80, channels) if reduce_here else (3, 16, 9, 8, channels)
+    outputs, grad, total = pl.pallas_call(
         functools.partial(kernel, n_gx, reduce_here),
         out_shape=(
-            jax.ShapeDtypeStruct((slots, voxels, channels), BF16),
-            jax.ShapeDtypeStruct((slots, voxels, channels), BF16),
-            jax.ShapeDtypeStruct((3, 3, 3, 16, 8, channels), F32),
+            results,
+            results,
+            jax.ShapeDtypeStruct(sums, jnp.int16 if reduce_here else F32),
         ),
-        in_specs=[smem, smem, any_space, any_space, vmem],
-        out_specs=(vmem, vmem, vmem),
+        in_specs=[smem, smem, any_space, any_space, any_space],
+        out_specs=(any_space, any_space, vmem),
         scratch_shapes=[
+            pltpu.VMEM((27, channels, channels), BF16),
+            pltpu.VMEM((slots, voxels, channels), BF16),
+            pltpu.VMEM((slots, voxels, channels), BF16),
             pltpu.VMEM((9 * slots + 1, 8, 64, channels), BF16),
             pltpu.VMEM((9 * slots + 1, 8, 64, channels), BF16),
             pltpu.VMEM((rows, 9 * channels), BF16),
@@ -405,11 +464,13 @@
             pltpu.VMEM((27 * channels, channels), BF16),
             pltpu.VMEM((3 * channels, 3 * channels), F32),
             pltpu.SMEM((slots, 27), jnp.int32),
-            pltpu.VMEM((3, 3, 3, 16, 8, channels), F32),
-            pltpu.VMEM((3, 3, 3, 8, 8, channels), F32),
-            pltpu.VMEM((3, 3, 3, 4, 8, channels), F32),
-            pltpu.VMEM((3, 3, 3, 3, 8, channels), F32),
-            pltpu.SemaphoreType.DMA((2,)),
+            pltpu.VMEM((3, 16, 9, 8, channels), F32),
+            pltpu.VMEM((3, 8, 9, 8, channels), F32),
+            pltpu.VMEM((3, 4, 80, channels), jnp.int16),
+            pltpu.VMEM((3, 4, 80, channels), jnp.int16),
+            pltpu.VMEM((3, 3, 80, channels), jnp.int16),
+            pltpu.VMEM((3, 3, 80, channels), jnp.int16),
+            pltpu.SemaphoreType.DMA((5,)),
             pltpu.SemaphoreType.DMA((2, 5)),
             pltpu.SemaphoreType.DMA((2, 5)),
             pltpu.SemaphoreType.DMA((3, 10)),
@@ -430,10 +491,21 @@
         cotangent.reshape(slots, 8, 64, channels),
         weights,
     )
-    weight_grad = weight_grad.reshape(27 * channels, channels)
     if not reduce_here:
-        weight_grad = lax.psum(weight_grad, ("gx", "gy"))
-    return outputs, grad, weight_grad
+        total = lax.psum(total, ("gx", "gy"))
+    outputs, grad, weight_grad = pl.pallas_call(
+        functools.partial(finish, reduce_here),
+        out_shape=(
+            results,
+            results,
+            jax.ShapeDtypeStruct((3, 3, 3, 16, 8, channels), F32),
+        ),
+        in_specs=[vmem, any_space, any_space],
+        out_specs=(any_space, any_space, vmem),
+        scratch_shapes=[pltpu.SemaphoreType.DMA((2, slots))],
+        compiler_params=pltpu.CompilerParams(vmem_limit_bytes=56 * 2**20),
+    )(total, outputs, grad)
+    return outputs, grad, weight_grad.reshape(27 * channels, channels)
 
 
 def solution(mesh):

time: 61.1 us -> 81.2 us (1.33)
  Pallas kernels: 54.5 us -> 79.7 us
  local copies, waits for them, and re-layouts: 5.08 us -> 0 us
    pallas_call x1 -> x2, Pallas kernels: 54.5 us -> 79.7 us  [the longest x1 44.4 us: body(): pl.pallas_call(functools.partial(kernel, n_gx, reduce_here), out_shape=(r...]
    unnamed x5 -> x0, local copies, waits for them, and re-layouts: 5.08 us -> none
where the time goes in v1:
time: 81.2 us; the launch traced here: 81 us
  Pallas kernels  79.7 us (98%)
  between operations  1.29 us (2%)
    pallas_call x1, Pallas kernels, body(): pl.pallas_call(functools.partial(kernel, n_gx, reduce_here), out_shape=(r...  44.4 us
    pallas_call x1, Pallas kernels, body(): pl.pallas_call(functools.partial(finish, reduce_here), out_shape=(results...  35.3 us

profile of v1, /device:TPU:0, one launch (start us, length us, event | category | flops | bytes accessed | tf_op | source)
XLA Modules:
  0.0 81.0 jit_solution(1280141541611933482)
XLA Ops:
  1.3 44.4 %shard_map.76 = (bf16[4,512,128]{2,1,0:T(8,128)(2,1)}, bf16[4,512,128]{2,1,0:T(8,128)(2,1)}, s16[3,16,80,128]{3,2,1,0:T(8,128)(2,1)}) custom-call(s32[4,27]{1,0:T(4,128)} %nb_ref.1, s32[1]{0:T(128)S(6)} %copy.8.counts_ref, bf16[4,8,64,128]{3,2,1,0:T(8,128)(2,1)} %bitcast.4, bf16[4,8,64,128]{3,2,1,0:T(8,128)(2,1)} %bitcast.5, bf16[27,128,128]{2,1,0:T(8,128)(2,1)} %w_hbm.1), custom_call_target="tpu_custom_call" | custom-call | flops 5435817984 | bytes 2097152 | tf_op jit(solution)/shard_map/pallas_call | solution.py:446
  45.7 35.3 %shard_map.77 = (bf16[4,512,128]{2,1,0:T(8,128)(2,1)}, bf16[4,512,128]{2,1,0:T(8,128)(2,1)}, f32[3,3,3,16,8,128]{5,4,3,2,1,0:T(8,128)}) custom-call(s16[3,16,80,128]{3,2,1,0:T(8,128)(2,1)} %get-tuple-element.9.q_ref, bf16[4,512,128]{2,1,0:T(8,128)(2,1)} %get-tuple-element.10.out_in, bf16[4,512,128]{2,1,0:T(8,128)(2,1)} %get-tuple-element.11.grad_in), custom_call_target="tpu_custom_call" | custom-call | tf_op jit(solution)/shard_map/pallas_call | solution.py:496

commit v2 on v1

--- a/solution.py
+++ b/solution.py
@@ -25,24 +25,47 @@
     return both[:9] * jnp.exp2(both[9:])
 
 
-def finish(coded, q_ref, out_in, grad_in, out_ref, grad_ref, dw_ref, sem):
-    copies = []
-    for n in range(out_in.shape[0]):
-        for k, (source, target) in enumerate(((out_in, out_ref), (grad_in, grad_ref))):
-            copies.append(pltpu.make_async_copy(source.at[n], target.at[n], sem.at[k, n]))
-    for copy in copies:
+def finish(
+    coded,
+    q_hbm,
+    out_in,
+    grad_in,
+    out_hbm,
+    grad_hbm,
+    dw_hbm,
+    q_ref,
+    out_ref,
+    grad_ref,
+    dw_ref,
+    in_sem,
+    out_sem,
+):
+    arrays = [(q_hbm.at[t], q_ref.at[t], dw_ref.at[:, t], dw_hbm.at[:, t]) for t in range(3)]
+    arrays += [(out_in, out_ref, out_ref, out_hbm), (grad_in, grad_ref, grad_ref, grad_hbm)]
+    inward = [
+        pltpu.make_async_copy(a[0], a[1], in_sem.at[k]) for k, a in enumerate(arrays)
+    ]
+    outward = [
+        pltpu.make_async_copy(a[2], a[3], out_sem.at[k]) for k, a in enumerate(arrays)
+    ]
+    for copy in inward:
         copy.start()
-
-    def piece(share, carry):
-        for t in range(3):
+    for t in range(3):
+        inward[t].wait()
+
+        def piece(share, carry):
             values = decode(q_ref[t, share]) if coded else q_ref[t, share]
             for a in range(3):
                 for c in range(3):
                     dw_ref[a, t, c, share] = values[a * 3 + c]
-        return carry
-
-    lax.fori_loop(0, 16, piece, 0)
-    for copy in copies:
+            return carry
+
+        lax.fori_loop(0, 16, piece, 0, unroll=4)
+        outward[t].start()
+    for k in (3, 4):
+        inward[k].wait()
+        outward[k].start()
+    for copy in outward:
         copy.wait()
 
 
@@ -262,7 +285,7 @@
 
         lax.fori_loop(0, slots, brick, 0)
 
-    def product(x_ref, weight, result):
+    def product(x_ref, weight, result, first, last):
         def brick(s, carry):
             total = jnp.zeros((512, 128), F32)
             for a in range(3):
@@ -275,7 +298,7 @@
             result[s] = jnp.where(s < counts_ref[0], total, 0.0).astype(BF16)
             return carry
 
-        lax.fori_loop(0, slots, brick, 0)
+        lax.fori_loop(first, last, brick, 0)
 
     def outer(t):
         acc[...] = jnp.zeros_like(acc)
@@ -299,6 +322,8 @@
 
     w_flat = w_ref.reshape(27 * 128, 128)
 
+    weights_in.wait()
+    lax.fori_loop(0, 27, turn, 0)
     arrived(0)
     start(1)
     build(table_f, x_f)
@@ -307,11 +332,9 @@
             outer(t)
         arrived(1)
         build(table_g, x_g)
-        weights_in.wait()
-        product(x_f, w_flat, out_ref)
+        product(x_f, w_flat, out_ref, 0, slots)
         out_copy.start()
-        lax.fori_loop(0, 27, turn, 0)
-        product(x_g, w_back, grad_ref)
+        product(x_g, w_back, grad_ref, 0, slots)
         grad_copy.start()
         out_copy.wait()
         grad_copy.wait()
@@ -406,17 +429,18 @@
     after_core(2)
     build(table_g, x_g)
     after_y(0)
-    weights_in.wait()
-    product(x_f, w_flat, out_ref)
+    mid = slots // 2
+    product(x_f, w_flat, out_ref, 0, mid)
+    after_y(1)
+    product(x_f, w_flat, out_ref, mid, slots)
     out_copy.start()
-    after_y(1)
     after_z(0)
     after_y(2)
-    lax.fori_loop(0, 27, turn, 0)
-    product(x_g, w_back, grad_ref)
-    grad_copy.start()
+    product(x_g, w_back, grad_ref, 0, mid)
     after_z(1)
     after_z_back(0)
+    product(x_g, w_back, grad_ref, mid, slots)
+    grad_copy.start()
     after_z(2)
     after_z_back(1)
     after_y_back(0)
@@ -500,9 +524,16 @@
             results,
             jax.ShapeDtypeStruct((3, 3, 3, 16, 8, channels), F32),
         ),
-        in_specs=[vmem, any_space, any_space],
-        out_specs=(any_space, any_space, vmem),
-        scratch_shapes=[pltpu.SemaphoreType.DMA((2, slots))],
+        in_specs=[any_space] * 3,
+        out_specs=(any_space,) * 3,
+        scratch_shapes=[
+            pltpu.VMEM(total.shape, total.dtype),
+            pltpu.VMEM((slots, voxels, channels), BF16),
+            pltpu.VMEM((slots, voxels, channels), BF16),
+            pltpu.VMEM((3, 3, 3, 16, 8, channels), F32),
+            pltpu.SemaphoreType.DMA((5,)),
+            pltpu.SemaphoreType.DMA((5,)),
+        ],
         compiler_params=pltpu.CompilerParams(vmem_limit_bytes=56 * 2**20),
     )(total, outputs, grad)
     return outputs, grad, weight_grad.reshape(27 * channels, channels)

time: 81.2 us -> 46.6 us (0.57)
  Pallas kernels: 79.7 us -> 45.1 us
    pallas_call x1, Pallas kernels: 35.3 us -> 2.69 us  [body(): pl.pallas_call(functools.partial(finish, reduce_here), out_shape=(results...]
    pallas_call x1, Pallas kernels: 44.4 us -> 42.4 us  [body(): pl.pallas_call(functools.partial(kernel, n_gx, reduce_here), out_shape=(r...]
where the time goes in v2:
time: 46.6 us; the launch traced here: 46.4 us
  Pallas kernels  45.1 us (97%)
  between operations  1.29 us (3%)
    pallas_call x1, Pallas kernels, body(): pl.pallas_call(functools.partial(kernel, n_gx, reduce_here), out_shape=(r...  42.4 us
    pallas_call x1, Pallas kernels, body(): pl.pallas_call(functools.partial(finish, reduce_here), out_shape=(results...  2.69 us

profile of v2, /device:TPU:0, one launch (start us, length us, event | category | flops | bytes accessed | tf_op | source)
XLA Modules:
  0.0 46.4 jit_solution(3889153057562490948)
XLA Ops:
  1.3 42.4 %shard_map.76 = (bf16[4,512,128]{2,1,0:T(8,128)(2,1)}, bf16[4,512,128]{2,1,0:T(8,128)(2,1)}, s16[3,16,80,128]{3,2,1,0:T(8,128)(2,1)}) custom-call(s32[4,27]{1,0:T(4,128)} %nb_ref.1, s32[1]{0:T(128)S(6)} %copy.8.counts_ref, bf16[4,8,64,128]{3,2,1,0:T(8,128)(2,1)} %bitcast.4, bf16[4,8,64,128]{3,2,1,0:T(8,128)(2,1)} %bitcast.5, bf16[27,128,128]{2,1,0:T(8,128)(2,1)} %w_hbm.1), custom_call_target="tpu_custom_call" | custom-call | flops 5435817984 | bytes 2097152 | tf_op jit(solution)/shard_map/pallas_call | solution.py:470
  43.7 2.7 %shard_map.77 = (bf16[4,512,128]{2,1,0:T(8,128)(2,1)}, bf16[4,512,128]{2,1,0:T(8,128)(2,1)}, f32[3,3,3,16,8,128]{5,4,3,2,1,0:T(8,128)}) custom-call(s16[3,16,80,128]{3,2,1,0:T(8,128)(2,1)} %get-tuple-element.9.q_hbm, bf16[4,512,128]{2,1,0:T(8,128)(2,1)} %get-tuple-element.10.out_in, bf16[4,512,128]{2,1,0:T(8,128)(2,1)} %get-tuple-element.11.grad_in), custom_call_target="tpu_custom_call" | custom-call | tf_op jit(solution)/shard_map/pallas_call | solution.py:520

commit v3 on v2

--- a/solution.py
+++ b/solution.py
@@ -301,19 +301,12 @@
         lax.fori_loop(first, last, brick, 0)
 
     def outer(t):
-        acc[...] = jnp.zeros_like(acc)
-
-        def brick(s, carry):
-            rows = pl.ds(pl.multiple_of(s * 640, 128), 640)
-            acc[...] += lax.dot_general(
-                x_f[rows, t * 384 : t * 384 + 384],
-                m_cat[rows, :],
-                (((0,), (0,)), ((), ())),
-                preferred_element_type=F32,
-            )
-            return carry
-
-        lax.fori_loop(0, slots, brick, 0)
+        acc[...] = lax.dot_general(
+            x_f[:, t * 384 : t * 384 + 384],
+            m_cat[...],
+            (((0,), (0,)), ((), ())),
+            preferred_element_type=F32,
+        )
         target = part if reduce_here else dw_ref
         for a in range(3):
             for c in range(3):

time: 46.6 us -> 44.4 us (0.953)
  Pallas kernels: 45.1 us -> 43 us
    pallas_call x1, Pallas kernels: 42.4 us -> 40.3 us  [body(): pl.pallas_call(functools.partial(kernel, n_gx, reduce_here), out_shape=(r...]
where the time goes in v3:
time: 44.4 us; the launch traced here: 44.3 us
  Pallas kernels  43 us (97%)
  between operations  1.29 us (3%)
    pallas_call x1, Pallas kernels, body(): pl.pallas_call(functools.partial(kernel, n_gx, reduce_here), out_shape=(r...  40.3 us
    pallas_call x1, Pallas kernels, body(): pl.pallas_call(functools.partial(finish, reduce_here), out_shape=(results...  2.69 us

profile of v3, /device:TPU:0, one launch (start us, length us, event | category | flops | bytes accessed | tf_op | source)
XLA Modules:
  0.0 44.3 jit_solution(1162823956261705450)
XLA Ops:
  1.3 40.3 %shard_map.76 = (bf16[4,512,128]{2,1,0:T(8,128)(2,1)}, bf16[4,512,128]{2,1,0:T(8,128)(2,1)}, s16[3,16,80,128]{3,2,1,0:T(8,128)(2,1)}) custom-call(s32[4,27]{1,0:T(4,128)} %nb_ref.1, s32[1]{0:T(128)S(6)} %copy.8.counts_ref, bf16[4,8,64,128]{3,2,1,0:T(8,128)(2,1)} %bitcast.4, bf16[4,8,64,128]{3,2,1,0:T(8,128)(2,1)} %bitcast.5, bf16[27,128,128]{2,1,0:T(8,128)(2,1)} %w_hbm.1), custom_call_target="tpu_custom_call" | custom-call | flops 5435817984 | bytes 2097152 | tf_op jit(solution)/shard_map/pallas_call | solution.py:463
  41.6 2.7 %shard_map.77 = (bf16[4,512,128]{2,1,0:T(8,128)(2,1)}, bf16[4,512,128]{2,1,0:T(8,128)(2,1)}, f32[3,3,3,16,8,128]{5,4,3,2,1,0:T(8,128)}) custom-call(s16[3,16,80,128]{3,2,1,0:T(8,128)(2,1)} %get-tuple-element.9.q_hbm, bf16[4,512,128]{2,1,0:T(8,128)(2,1)} %get-tuple-element.10.out_in, bf16[4,512,128]{2,1,0:T(8,128)(2,1)} %get-tuple-element.11.grad_in), custom_call_target="tpu_custom_call" | custom-call | tf_op jit(solution)/shard_map/pallas_call | solution.py:513
